TPU v7x, 32 devices: a whole 2x2x4 slice. The times are simulated.
32 devices in a mesh: segment: 2 (over core), inline: 4 (over z), xline: 4 (over y, x).
Axes of the slice: x: 2, y: 2, z: 4, core: 2. Of those that a mesh axis runs over, the one named last changes fastest.
Arguments:
- survey: float32 [2, 16, 16, 1024], P(None, 'inline', 'xline'), may hold values from -6 to 6
- conduct: bfloat16 [3, 2, 16, 16, 1024], P(None, None, 'inline', 'xline'), may hold values from 0.099609375 to 1
- widths: int32 [2, 4], P(None, 'inline'), may hold values from 2 to 4, as said below
Outputs:
- coherence: float32 [2, 16, 16, 1024], P('segment', 'inline', 'xline')
- curvature: float32 [2, 16, 16, 1024], P('segment', 'inline', 'xline')
Inputs may be any that keep to these rules, and one draw needn't show every extreme that they name: `widths`: in every micro-batch some device holds exactly 4 live rows and another exactly 2.
All inputs are finite; a program needn't handle non-finite values.
Results may differ from a plain program's by a relative error of at most 0.0003.
Values sent between devices are 32-bit elements; how exact they have to be, the bound alone decides.
A program may use at most 64 MiB of HBM per device.

v0:
```python
import jax
import jax.numpy as jnp
from jax import lax
from jax.sharding import PartitionSpec as P

STEPS = 2


step_size = 0.15
epsilon = 1e-06


def extended(value, sides, width):
    for axis, dim in sides:
        count, length = (lax.axis_size(axis), value.shape[dim])
        up = [(i, (i + 1) % count) for i in range(count - 1)]
        down = [(j, i) for i, j in up]
        last = lax.slice_in_dim(value, length - width, length, axis=dim)
        initial = lax.slice_in_dim(value, 0, width, axis=dim)
        before = lax.ppermute(last, axis, up)
        after = lax.ppermute(initial, axis, down)
        value = jnp.concatenate([before, value, after], axis=dim)
    return value


def shifted_2(value, axis, steps):
    count = lax.axis_size(axis)
    initial, last = (max(0, -steps), min(count, count - steps))
    return lax.ppermute(value, axis, [(source, source + steps) for source in range(initial, last)])


def shifted(source, which_axis, offset):
    length = source.shape[which_axis]
    margins = [(0, 0)] * source.ndim
    if offset > 0:
        margins[which_axis] = (0, offset)
        padded = jnp.pad(source, margins)
        return lax.slice_in_dim(padded, offset, offset + length, axis=which_axis)
    margins[which_axis] = (-offset, 0)
    padded = jnp.pad(source, margins)
    return lax.slice_in_dim(padded, 0, length, axis=which_axis)


def neighbor(source, which_axis, offset, opened):
    return jnp.where(opened, shifted(source, which_axis, offset), source)


def face_masks(depth, width, rows, cols, samples):
    inline_pos = lax.axis_index("inline")
    inline_count = lax.axis_size("inline")
    xline_pos = lax.axis_index("xline")
    xline_count = lax.axis_size("xline")
    own_row = jnp.arange(rows + 2 * depth, dtype=jnp.int32) - depth
    first_row = inline_pos == 0
    last_row = inline_pos == inline_count - 1
    row_up = jnp.logical_not(last_row & (own_row == width - 1) | first_row & (own_row == -1))
    row_down = jnp.logical_not(last_row & (own_row == width) | first_row & (own_row == 0))
    own_col = jnp.arange(cols + 2 * depth, dtype=jnp.int32) - depth
    first_col = xline_pos == 0
    last_col = xline_pos == xline_count - 1
    col_up = jnp.logical_not(last_col & (own_col == cols - 1) | first_col & (own_col == -1))
    col_down = jnp.logical_not(last_col & (own_col == cols) | first_col & (own_col == 0))
    sample = jnp.arange(samples, dtype=jnp.int32)
    return [
        (row_up[:, None, None], row_down[:, None, None]),
        (col_up[None, :, None], col_down[None, :, None]),
        ((sample < samples - 1)[None, None, :], (sample > 0)[None, None, :]),
    ]


def extend(field, depth, width):
    spread = extended(field, (("xline", 2),), depth)
    upper_rows = lax.dynamic_slice_in_dim(spread, width - depth, depth, 1)
    lower_rows = spread[:, :depth]
    from_lower = shifted_2(upper_rows, "inline", 1)
    from_upper = shifted_2(lower_rows, "inline", -1)
    padded = jnp.pad(spread, ((0, 0), (0, depth), (0, 0), (0, 0)))
    padded = lax.dynamic_update_slice_in_dim(padded, from_upper, width, 1)
    return jnp.concatenate([from_lower, padded], 1)


def relax_step(values, coeffs, masks):
    change = jnp.zeros_like(values)
    for which_axis in range(3):
        kk = coeffs[which_axis]
        up_open, down_open = masks[which_axis]
        for offset, opened in ((1, up_open), (-1, down_open)):
            change = change + 0.5 * (kk + neighbor(kk, which_axis, offset, opened)) * (
                neighbor(values, which_axis, offset, opened) - values
            )
    return values + step_size * change


def diffuse(field, conduct_batch, width):
    rows, cols, samples = field.shape
    rounds = [(1, 1)] * STEPS
    coeffs_own = conduct_batch.astype(jnp.float32)
    for depth, count in rounds:
        grown = extend(jnp.concatenate([field[None], coeffs_own], 0), depth, width)
        masks = face_masks(depth, width, rows, cols, samples)
        values = grown[0]
        coeffs = grown[1:]
        values = relax_step(values, coeffs, masks)
        field = values[depth : depth + rows, depth : depth + cols]
    return field


def attributes(smooth, width):
    rows, cols, samples = smooth.shape
    grown = extend(smooth[None], 2, width)[0]
    masks = face_masks(2, width, rows, cols, samples)
    grads = []
    for which_axis in range(3):
        up_open, down_open = masks[which_axis]
        grads.append(
            0.5
            * (neighbor(grown, which_axis, 1, up_open) - neighbor(grown, which_axis, -1, down_open))
        )
    seconds = []
    for which_axis in range(2):
        up_open, down_open = masks[which_axis]
        seconds.append(
            neighbor(grown, which_axis, 1, up_open)
            + neighbor(grown, which_axis, -1, down_open)
            - 2.0 * grown
        )
    combos = [(0, 0), (1, 1), (2, 2), (0, 1), (0, 2), (1, 2)]
    tensor = jnp.stack(
        [grads[first_index] * grads[second_index] for first_index, second_index in combos], 0
    )
    for which_axis in range(3):
        up_open, down_open = masks[which_axis]
        tensor = 0.25 * (
            neighbor(tensor, which_axis + 1, 1, up_open)
            + 2.0 * tensor
            + neighbor(tensor, which_axis + 1, -1, down_open)
        )
    trace = tensor[0] + tensor[1] + tensor[2]
    minors = (
        tensor[0] * tensor[1]
        - tensor[3] * tensor[3]
        + tensor[0] * tensor[2]
        - tensor[4] * tensor[4]
        + tensor[1] * tensor[2]
        - tensor[5] * tensor[5]
    )
    coherence = 1.0 - 3.0 * minors / (trace * trace + epsilon)
    curvature = (seconds[0] + seconds[1]) / (1.0 + grads[0] * grads[0] + grads[1] * grads[1]) ** 1.5
    outcome = jnp.stack([coherence, curvature], 0)[:, 2 : 2 + rows, 2 : 2 + cols]
    live_rows = (jnp.arange(rows, dtype=jnp.int32) < width)[None, :, None, None]
    return jnp.where(live_rows, outcome, 0.0)


def on_device(survey, conduct, widths):
    segment_pos = lax.axis_index("segment")
    batches = survey.shape[0]
    results = []
    for batch in range(batches):
        picked = (batch + segment_pos) % batches
        own_field = lax.dynamic_index_in_dim(survey, picked, 0, keepdims=False)
        own_coeffs = lax.dynamic_index_in_dim(conduct, picked, 1, keepdims=False)
        own_width = lax.dynamic_index_in_dim(widths[:, 0], picked, 0, keepdims=False)
        smooth = diffuse(own_field, own_coeffs, own_width)
        arrived = shifted_2(smooth, "segment", 1)
        results.append(attributes(arrived, widths[batch, 0]))
    returned = shifted_2(results[0], "segment", -1)
    chosen = jnp.where(segment_pos == 0, returned, results[1])
    return (chosen[0][None], chosen[1][None])


def solution(mesh):
    placed = (
        P(None, "inline", "xline", None),
        P(None, None, "inline", "xline", None),
        P(None, "inline"),
    )
    return jax.shard_map(
        on_device,
        mesh=mesh,
        in_specs=placed,
        out_specs=(P("segment", "inline", "xline", None), P("segment", "inline", "xline", None)),
        check_vma=False,
    )
```

profile of v0, /device:TPU:0, one launch (start us, length us, event | category | flops | bytes accessed | tf_op | source)
XLA Modules:
  0.0 131.5 jit_solution(8838744787979808839)
XLA Ops:
  2.7 4.8 %collective-permute-start.14 = (f32[4,4,1,1024]{3,2,1,0:T(1,128)S(1)}, f32[4,4,1,1024]{3,2,1,0:T(1,128)S(1)}, u32[]{:S(2)}, u32[]{:S(2)}) collective-permute-start(f32[4,4,1,1024]{3,2,1,0:T(1,128)S(1)} %get-tuple-element.40), channel_id=1, source_target_pairs={{0,1},{1,2},{2,3},{4,5},{5,6},{6,7},{8,9},{9,10},{10,11},{12,13},{... | collective-permute-start | bytes 196616 | tf_op jit(solution)/shard_map/ppermute | solution.py:20
  8.9 4.5 %collective-permute-start = (f32[4,4,1,1024]{3,2,1,0:T(1,128)S(1)}, f32[4,4,1,1024]{3,2,1,0:T(1,128)S(1)}, u32[]{:S(2)}, u32[]{:S(2)}) collective-permute-start(f32[4,4,1,1024]{3,2,1,0:T(1,128)S(1)} %get-tuple-element.44), channel_id=1, source_target_pairs={{0,1},{1,2},{2,3},{4,5},{5,6},{6,7},{8,9},{9,10},{10,11},{12,13},{... | collective-permute-start | bytes 196616 | tf_op jit(solution)/shard_map/ppermute | solution.py:20
  35.8 4.6 %collective-permute-start.2 = (f32[4,1,6,1024]{3,2,1,0:T(8,128)S(1)}, f32[4,1,6,1024]{3,2,1,0:T(8,128)S(1)}, u32[]{:S(2)}, u32[]{:S(2)}) collective-permute-start(f32[4,1,6,1024]{3,2,1,0:T(8,128)S(1)} %get-tuple-element.36), channel_id=1, source_target_pairs={{0,4},{4,8},{8,12},{1,5},{5,9},{9,13},{2,6},{6,10},{10,14},{3,7},{... | collective-permute-start | bytes 294920 | tf_op jit(solution)/shard_map/ppermute | solution.py:29
  40.4 1.3 collective-permute-start.3
  41.7 4.6 %collective-permute-start.16 = (f32[4,1,6,1024]{3,2,1,0:T(8,128)S(1)}, f32[4,1,6,1024]{3,2,1,0:T(8,128)S(1)}, u32[]{:S(2)}, u32[]{:S(2)}) collective-permute-start(f32[4,1,6,1024]{3,2,1,0:T(8,128)S(1)} %get-tuple-element.32), channel_id=1, source_target_pairs={{0,4},{4,8},{8,12},{1,5},{5,9},{9,13},{2,6},{6,10},{10,14},{3,7},{... | collective-permute-start | bytes 294920 | tf_op jit(solution)/shard_map/ppermute | solution.py:29
  46.3 2.5 %collective-permute-done.16 = f32[4,1,6,1024]{3,2,1,0:T(8,128)S(1)} collective-permute-done((f32[4,1,6,1024]{3,2,1,0:T(8,128)S(1)}, f32[4,1,6,1024]{3,2,1,0:T(8,128)S(1)}, u32[]{:S(2)}, u32[]{:S(2)}) %collective-permute-start.16) | collective-permute-done | bytes 98336 | tf_op jit(solution)/shard_map/ppermute | solution.py:29
  49.6 4.9 %collective-permute-start.18 = (f32[4,4,1,1024]{3,2,1,0:T(1,128)S(1)}, f32[4,4,1,1024]{3,2,1,0:T(1,128)S(1)}, u32[]{:S(2)}, u32[]{:S(2)}) collective-permute-start(f32[4,4,1,1024]{3,2,1,0:T(1,128)S(1)} %get-tuple-element.38), channel_id=1, source_target_pairs={{0,1},{1,2},{2,3},{4,5},{5,6},{6,7},{8,9},{9,10},{10,11},{12,13},{... | collective-permute-start | bytes 196616 | tf_op jit(solution)/shard_map/ppermute | solution.py:20
  56.4 5.2 %collective-permute-done.19 = f32[4,4,1,1024]{3,2,1,0:T(1,128)S(1)} collective-permute-done((f32[4,4,1,1024]{3,2,1,0:T(1,128)S(1)}, f32[4,4,1,1024]{3,2,1,0:T(1,128)S(1)}, u32[]{:S(2)}, u32[]{:S(2)}) %collective-permute-start.19) | collective-permute-done | bytes 65568 | tf_op jit(solution)/shard_map/ppermute | solution.py:21
  63.5 5.0 %collective-permute-start.20 = (f32[4,1,6,1024]{3,2,1,0:T(8,128)S(1)}, f32[4,1,6,1024]{3,2,1,0:T(8,128)S(1)}, u32[]{:S(2)}, u32[]{:S(2)}) collective-permute-start(f32[4,1,6,1024]{3,2,1,0:T(8,128)S(1)} %get-tuple-element.30), channel_id=1, source_target_pairs={{0,4},{4,8},{8,12},{1,5},{5,9},{9,13},{2,6},{6,10},{10,14},{3,7},{... | collective-permute-start | bytes 294920 | tf_op jit(solution)/shard_map/ppermute | solution.py:29
  69.1 1.8 %collective-permute-done.20 = f32[4,1,6,1024]{3,2,1,0:T(8,128)S(1)} collective-permute-done((f32[4,1,6,1024]{3,2,1,0:T(8,128)S(1)}, f32[4,1,6,1024]{3,2,1,0:T(8,128)S(1)}, u32[]{:S(2)}, u32[]{:S(2)}) %collective-permute-start.20) | collective-permute-done | bytes 98336 | tf_op jit(solution)/shard_map/ppermute | solution.py:29
  71.8 1.3 collective-permute-start.22
  73.4 4.8 %collective-permute-start.4 = (f32[4,4,1,1024]{3,2,1,0:T(1,128)S(1)}, f32[4,4,1,1024]{3,2,1,0:T(1,128)S(1)}, u32[]{:S(2)}, u32[]{:S(2)}) collective-permute-start(f32[4,4,1,1024]{3,2,1,0:T(1,128)S(1)} %get-tuple-element.42), channel_id=1, source_target_pairs={{0,1},{1,2},{2,3},{4,5},{5,6},{6,7},{8,9},{9,10},{10,11},{12,13},{... | collective-permute-start | bytes 196616 | tf_op jit(solution)/shard_map/ppermute | solution.py:20
  79.6 4.5 %collective-permute-start.23 = (f32[1,4,2,1024]{3,2,1,0:T(2,128)S(1)}, f32[1,4,2,1024]{3,2,1,0:T(2,128)S(1)}, u32[]{:S(2)}, u32[]{:S(2)}) collective-permute-start(f32[1,4,2,1024]{3,2,1,0:T(2,128)S(1)} %get-tuple-element.88), channel_id=1, source_target_pairs={{0,1},{1,2},{2,3},{4,5},{5,6},{6,7},{8,9},{9,10},{10,11},{12,13},{... | collective-permute-start | bytes 98312 | tf_op jit(solution)/shard_map/ppermute | solution.py:20
  85.7 4.4 %collective-permute-start.6 = (f32[4,1,6,1024]{3,2,1,0:T(8,128)S(1)}, f32[4,1,6,1024]{3,2,1,0:T(8,128)S(1)}, u32[]{:S(2)}, u32[]{:S(2)}) collective-permute-start(f32[4,1,6,1024]{3,2,1,0:T(8,128)S(1)} %get-tuple-element.34), channel_id=1, source_target_pairs={{0,4},{4,8},{8,12},{1,5},{5,9},{9,13},{2,6},{6,10},{10,14},{3,7},{... | collective-permute-start | bytes 294920 | tf_op jit(solution)/shard_map/ppermute | solution.py:29
  91.5 4.5 %collective-permute-start.25 = (f32[1,2,8,1024]{3,2,1,0:T(8,128)S(1)}, f32[1,2,8,1024]{3,2,1,0:T(8,128)S(1)}, u32[]{:S(2)}, u32[]{:S(2)}) collective-permute-start(f32[1,2,8,1024]{3,2,1,0:T(8,128)S(1)} %get-tuple-element.82), channel_id=1, source_target_pairs={{0,4},{4,8},{8,12},{1,5},{5,9},{9,13},{2,6},{6,10},{10,14},{3,7},{... | collective-permute-start | bytes 196616 | tf_op jit(solution)/shard_map/ppermute | solution.py:29
  98.2 1.3 collective-permute-start.8
  99.5 2.8 %collective-permute-done.26 = f32[1,2,8,1024]{3,2,1,0:T(8,128)S(1)} collective-permute-done((f32[1,2,8,1024]{3,2,1,0:T(8,128)S(1)}, f32[1,2,8,1024]{3,2,1,0:T(8,128)S(1)}, u32[]{:S(2)}, u32[]{:S(2)}) %collective-permute-start.26) | collective-permute-done | bytes 65568 | tf_op jit(solution)/shard_map/ppermute | solution.py:29
  102.3 4.5 %collective-permute-start.9 = (f32[1,4,2,1024]{3,2,1,0:T(2,128)S(1)}, f32[1,4,2,1024]{3,2,1,0:T(2,128)S(1)}, u32[]{:S(2)}, u32[]{:S(2)}) collective-permute-start(f32[1,4,2,1024]{3,2,1,0:T(2,128)S(1)} %get-tuple-element.90), channel_id=1, source_target_pairs={{0,1},{1,2},{2,3},{4,5},{5,6},{6,7},{8,9},{9,10},{10,11},{12,13},{... | collective-permute-start | bytes 98312 | tf_op jit(solution)/shard_map/ppermute | solution.py:20
  108.4 4.2 %collective-permute-done.10 = f32[1,4,2,1024]{3,2,1,0:T(2,128)S(1)} collective-permute-done((f32[1,4,2,1024]{3,2,1,0:T(2,128)S(1)}, f32[1,4,2,1024]{3,2,1,0:T(2,128)S(1)}, u32[]{:S(2)}, u32[]{:S(2)}) %collective-permute-start.10) | collective-permute-done | bytes 32800 | tf_op jit(solution)/shard_map/ppermute | solution.py:21
  114.2 4.7 %collective-permute-start.11 = (f32[1,2,8,1024]{3,2,1,0:T(8,128)S(1)}, f32[1,2,8,1024]{3,2,1,0:T(8,128)S(1)}, u32[]{:S(2)}, u32[]{:S(2)}) collective-permute-start(f32[1,2,8,1024]{3,2,1,0:T(8,128)S(1)} %get-tuple-element.86), channel_id=1, source_target_pairs={{0,4},{4,8},{8,12},{1,5},{5,9},{9,13},{2,6},{6,10},{10,14},{3,7},{... | collective-permute-start | bytes 196616 | tf_op jit(solution)/shard_map/ppermute | solution.py:29
  119.0 1.7 %collective-permute-done.11 = f32[1,2,8,1024]{3,2,1,0:T(8,128)S(1)} collective-permute-done((f32[1,2,8,1024]{3,2,1,0:T(8,128)S(1)}, f32[1,2,8,1024]{3,2,1,0:T(8,128)S(1)}, u32[]{:S(2)}, u32[]{:S(2)}) %collective-permute-start.11) | collective-permute-done | bytes 65568 | tf_op jit(solution)/shard_map/ppermute | solution.py:29
  123.9 1.6 %broadcast_multiply_fusion = (f32[6,8,8,1024]{3,2,1,0:T(8,128)S(1)}, f32[6,8,8,1024]{3,2,1,0:T(8,128)S(1)}, f32[6,8,8,1024]{3,2,1,0:T(8,128)S(1)}, f32[6,8,8,1024]{3,2,1,0:T(8,128)S(1)}) fusion(f32[6,8,8,1024]{3,2,1,0:T(8,128)S(1)} %get-tuple-element.4, pred[8]{0:T(512)(128)(4,1)S(1)} %get-tuple-element.111, f32[6,8,8,1024]{3,2,1,0:T(8,128)S(1)} %get-tuple-element.5, ...), kind=kLoop, calls=%fused_computation.62 | loop fusion | flops 4718592 | bytes 12582928 | tf_op jit(solution)/shard_map/mul | solution.py:133
  125.6 1.7 %fusion.16 = (f32[6,8,8,1024]{3,2,1,0:T(8,128)S(1)}, f32[6,8,8,1024]{3,2,1,0:T(8,128)S(1)}) fusion(f32[6,8,8,1024]{3,2,1,0:T(8,128)S(1)} %get-tuple-element.2, f32[6,8,8,1024]{3,2,1,0:T(8,128)S(1)} %get-tuple-element.3, pred[1024]{0:T(1024)(128)(4,1)S(1)} %get-tuple-element.118, pred[1024]{0:T(1024)(128)(4,1)S(1)} %get-tuple-element.119, ...), kind=kLoop, calls=%fused_computation.28 | loop fusion | flops 4718592 | bytes 9439232 | tf_op jit(solution)/shard_map/mul | solution.py:133
  129.0 1.8 %collective-permute-done.13 = f32[2,4,4,1024]{3,2,1,0:T(4,128)S(1)} collective-permute-done((f32[2,4,4,1024]{3,2,1,0:T(4,128)S(1)}, f32[2,4,4,1024]{3,2,1,0:T(4,128)S(1)}, u32[]{:S(2)}, u32[]{:S(2)}) %collective-permute-start.13) | collective-permute-done | bytes 131104 | tf_op jit(solution)/shard_map/ppermute | solution.py:29
  (111 shorter events, 32.6 us)
Async XLA Ops:
  2.7 31.2 %collective-permute-start.14 = (f32[4,4,1,1024]{3,2,1,0:T(1,128)S(1)}, f32[4,4,1,1024]{3,2,1,0:T(1,128)S(1)}, u32[]{:S(2)}, u32[]{:S(2)}) collective-permute-start(f32[4,4,1,1024]{3,2,1,0:T(1,128)S(1)} %get-tuple-element.40), channel_id=1, source_target_pairs={{0,1},{1,2},{2,3},{4,5},{5,6},{6,7},{8,9},{9,10},{10,11},{12,13},{... | collective-permute-start | bytes 196616 | tf_op jit(solution)/shard_map/ppermute | solution.py:20
  7.5 26.4 %collective-permute-start.15 = (f32[4,4,1,1024]{3,2,1,0:T(1,128)S(1)}, f32[4,4,1,1024]{3,2,1,0:T(1,128)S(1)}, u32[]{:S(2)}, u32[]{:S(2)}) collective-permute-start(f32[4,4,1,1024]{3,2,1,0:T(1,128)S(1)} %get-tuple-element.41), channel_id=1, source_target_pairs={{1,0},{2,1},{3,2},{5,4},{6,5},{7,6},{9,8},{10,9},{11,10},{13,12},{... | collective-permute-start | bytes 196616 | tf_op jit(solution)/shard_map/ppermute | solution.py:21
  8.9 26.5 %collective-permute-start = (f32[4,4,1,1024]{3,2,1,0:T(1,128)S(1)}, f32[4,4,1,1024]{3,2,1,0:T(1,128)S(1)}, u32[]{:S(2)}, u32[]{:S(2)}) collective-permute-start(f32[4,4,1,1024]{3,2,1,0:T(1,128)S(1)} %get-tuple-element.44), channel_id=1, source_target_pairs={{0,1},{1,2},{2,3},{4,5},{5,6},{6,7},{8,9},{9,10},{10,11},{12,13},{... | collective-permute-start | bytes 196616 | tf_op jit(solution)/shard_map/ppermute | solution.py:20
  13.5 22.0 %collective-permute-start.1 = (f32[4,4,1,1024]{3,2,1,0:T(1,128)S(1)}, f32[4,4,1,1024]{3,2,1,0:T(1,128)S(1)}, u32[]{:S(2)}, u32[]{:S(2)}) collective-permute-start(f32[4,4,1,1024]{3,2,1,0:T(1,128)S(1)} %get-tuple-element.45), channel_id=1, source_target_pairs={{1,0},{2,1},{3,2},{5,4},{6,5},{7,6},{9,8},{10,9},{11,10},{13,12},{... | collective-permute-start | bytes 196616 | tf_op jit(solution)/shard_map/ppermute | solution.py:21
  34.1 12.1 %collective-permute-start.17 = (f32[4,1,6,1024]{3,2,1,0:T(8,128)S(1)}, f32[4,1,6,1024]{3,2,1,0:T(8,128)S(1)}, u32[]{:S(2)}, u32[]{:S(2)}) collective-permute-start(f32[4,1,6,1024]{3,2,1,0:T(8,128)S(1)} %get-tuple-element.33), channel_id=1, source_target_pairs={{4,0},{8,4},{12,8},{5,1},{9,5},{13,9},{6,2},{10,6},{14,10},{7,3},{... | collective-permute-start | bytes 294920 | tf_op jit(solution)/shard_map/ppermute | solution.py:29
  35.8 20.1 %collective-permute-start.2 = (f32[4,1,6,1024]{3,2,1,0:T(8,128)S(1)}, f32[4,1,6,1024]{3,2,1,0:T(8,128)S(1)}, u32[]{:S(2)}, u32[]{:S(2)}) collective-permute-start(f32[4,1,6,1024]{3,2,1,0:T(8,128)S(1)} %get-tuple-element.36), channel_id=1, source_target_pairs={{0,4},{4,8},{8,12},{1,5},{5,9},{9,13},{2,6},{6,10},{10,14},{3,7},{... | collective-permute-start | bytes 294920 | tf_op jit(solution)/shard_map/ppermute | solution.py:29
  40.4 15.5 %collective-permute-start.3 = (f32[4,1,6,1024]{3,2,1,0:T(8,128)S(1)}, f32[4,1,6,1024]{3,2,1,0:T(8,128)S(1)}, u32[]{:S(2)}, u32[]{:S(2)}) collective-permute-start(f32[4,1,6,1024]{3,2,1,0:T(8,128)S(1)} %get-tuple-element.37), channel_id=1, source_target_pairs={{4,0},{8,4},{12,8},{5,1},{9,5},{13,9},{6,2},{10,6},{14,10},{7,3},{... | collective-permute-start | bytes 294920 | tf_op jit(solution)/shard_map/ppermute | solution.py:29
  41.7 7.1 %collective-permute-start.16 = (f32[4,1,6,1024]{3,2,1,0:T(8,128)S(1)}, f32[4,1,6,1024]{3,2,1,0:T(8,128)S(1)}, u32[]{:S(2)}, u32[]{:S(2)}) collective-permute-start(f32[4,1,6,1024]{3,2,1,0:T(8,128)S(1)} %get-tuple-element.32), channel_id=1, source_target_pairs={{0,4},{4,8},{8,12},{1,5},{5,9},{9,13},{2,6},{6,10},{10,14},{3,7},{... | collective-permute-start | bytes 294920 | tf_op jit(solution)/shard_map/ppermute | solution.py:29
  49.6 6.8 %collective-permute-start.18 = (f32[4,4,1,1024]{3,2,1,0:T(1,128)S(1)}, f32[4,4,1,1024]{3,2,1,0:T(1,128)S(1)}, u32[]{:S(2)}, u32[]{:S(2)}) collective-permute-start(f32[4,4,1,1024]{3,2,1,0:T(1,128)S(1)} %get-tuple-element.38), channel_id=1, source_target_pairs={{0,1},{1,2},{2,3},{4,5},{5,6},{6,7},{8,9},{9,10},{10,11},{12,13},{... | collective-permute-start | bytes 196616 | tf_op jit(solution)/shard_map/ppermute | solution.py:20
  54.5 7.1 %collective-permute-start.19 = (f32[4,4,1,1024]{3,2,1,0:T(1,128)S(1)}, f32[4,4,1,1024]{3,2,1,0:T(1,128)S(1)}, u32[]{:S(2)}, u32[]{:S(2)}) collective-permute-start(f32[4,4,1,1024]{3,2,1,0:T(1,128)S(1)} %get-tuple-element.39), channel_id=1, source_target_pairs={{1,0},{2,1},{3,2},{5,4},{6,5},{7,6},{9,8},{10,9},{11,10},{13,12},{... | collective-permute-start | bytes 196616 | tf_op jit(solution)/shard_map/ppermute | solution.py:21
  61.8 7.3 %collective-permute-start.21 = (f32[4,1,6,1024]{3,2,1,0:T(8,128)S(1)}, f32[4,1,6,1024]{3,2,1,0:T(8,128)S(1)}, u32[]{:S(2)}, u32[]{:S(2)}) collective-permute-start(f32[4,1,6,1024]{3,2,1,0:T(8,128)S(1)} %get-tuple-element.31), channel_id=1, source_target_pairs={{4,0},{8,4},{12,8},{5,1},{9,5},{13,9},{6,2},{10,6},{14,10},{7,3},{... | collective-permute-start | bytes 294920 | tf_op jit(solution)/shard_map/ppermute | solution.py:29
  63.5 7.5 %collective-permute-start.20 = (f32[4,1,6,1024]{3,2,1,0:T(8,128)S(1)}, f32[4,1,6,1024]{3,2,1,0:T(8,128)S(1)}, u32[]{:S(2)}, u32[]{:S(2)}) collective-permute-start(f32[4,1,6,1024]{3,2,1,0:T(8,128)S(1)} %get-tuple-element.30), channel_id=1, source_target_pairs={{0,4},{4,8},{8,12},{1,5},{5,9},{9,13},{2,6},{6,10},{10,14},{3,7},{... | collective-permute-start | bytes 294920 | tf_op jit(solution)/shard_map/ppermute | solution.py:29
  71.8 7.7 %collective-permute-start.22 = (f32[4,4,1024]{2,1,0:T(4,128)S(1)}, f32[4,4,1024]{2,1,0:T(4,128)S(1)}, u32[]{:S(2)}, u32[]{:S(2)}) collective-permute-start(f32[4,4,1024]{2,1,0:T(4,128)S(1)} %fusion.154), channel_id=1, source_target_pairs={{0,16},{1,17},{2,18},{3,19},{4,20},{5,21},{6,22},{7,23},{8,24},{9,... | collective-permute-start | bytes 196616 | tf_op jit(solution)/shard_map/ppermute | solution.py:29
  73.4 12.0 %collective-permute-start.4 = (f32[4,4,1,1024]{3,2,1,0:T(1,128)S(1)}, f32[4,4,1,1024]{3,2,1,0:T(1,128)S(1)}, u32[]{:S(2)}, u32[]{:S(2)}) collective-permute-start(f32[4,4,1,1024]{3,2,1,0:T(1,128)S(1)} %get-tuple-element.42), channel_id=1, source_target_pairs={{0,1},{1,2},{2,3},{4,5},{5,6},{6,7},{8,9},{9,10},{10,11},{12,13},{... | collective-permute-start | bytes 196616 | tf_op jit(solution)/shard_map/ppermute | solution.py:20
  78.2 7.2 %collective-permute-start.5 = (f32[4,4,1,1024]{3,2,1,0:T(1,128)S(1)}, f32[4,4,1,1024]{3,2,1,0:T(1,128)S(1)}, u32[]{:S(2)}, u32[]{:S(2)}) collective-permute-start(f32[4,4,1,1024]{3,2,1,0:T(1,128)S(1)} %get-tuple-element.43), channel_id=1, source_target_pairs={{1,0},{2,1},{3,2},{5,4},{6,5},{7,6},{9,8},{10,9},{11,10},{13,12},{... | collective-permute-start | bytes 196616 | tf_op jit(solution)/shard_map/ppermute | solution.py:21
  79.6 11.8 %collective-permute-start.23 = (f32[1,4,2,1024]{3,2,1,0:T(2,128)S(1)}, f32[1,4,2,1024]{3,2,1,0:T(2,128)S(1)}, u32[]{:S(2)}, u32[]{:S(2)}) collective-permute-start(f32[1,4,2,1024]{3,2,1,0:T(2,128)S(1)} %get-tuple-element.88), channel_id=1, source_target_pairs={{0,1},{1,2},{2,3},{4,5},{5,6},{6,7},{8,9},{9,10},{10,11},{12,13},{... | collective-permute-start | bytes 98312 | tf_op jit(solution)/shard_map/ppermute | solution.py:20
  84.1 7.3 %collective-permute-start.24 = (f32[1,4,2,1024]{3,2,1,0:T(2,128)S(1)}, f32[1,4,2,1024]{3,2,1,0:T(2,128)S(1)}, u32[]{:S(2)}, u32[]{:S(2)}) collective-permute-start(f32[1,4,2,1024]{3,2,1,0:T(2,128)S(1)} %get-tuple-element.89), channel_id=1, source_target_pairs={{1,0},{2,1},{3,2},{5,4},{6,5},{7,6},{9,8},{10,9},{11,10},{13,12},{... | collective-permute-start | bytes 98312 | tf_op jit(solution)/shard_map/ppermute | solution.py:21
  85.7 11.7 %collective-permute-start.6 = (f32[4,1,6,1024]{3,2,1,0:T(8,128)S(1)}, f32[4,1,6,1024]{3,2,1,0:T(8,128)S(1)}, u32[]{:S(2)}, u32[]{:S(2)}) collective-permute-start(f32[4,1,6,1024]{3,2,1,0:T(8,128)S(1)} %get-tuple-element.34), channel_id=1, source_target_pairs={{0,4},{4,8},{8,12},{1,5},{5,9},{9,13},{2,6},{6,10},{10,14},{3,7},{... | collective-permute-start | bytes 294920 | tf_op jit(solution)/shard_map/ppermute | solution.py:29
  90.1 7.3 %collective-permute-start.7 = (f32[4,1,6,1024]{3,2,1,0:T(8,128)S(1)}, f32[4,1,6,1024]{3,2,1,0:T(8,128)S(1)}, u32[]{:S(2)}, u32[]{:S(2)}) collective-permute-start(f32[4,1,6,1024]{3,2,1,0:T(8,128)S(1)} %get-tuple-element.35), channel_id=1, source_target_pairs={{4,0},{8,4},{12,8},{5,1},{9,5},{13,9},{6,2},{10,6},{14,10},{7,3},{... | collective-permute-start | bytes 294920 | tf_op jit(solution)/shard_map/ppermute | solution.py:29
  91.5 16.6 %collective-permute-start.25 = (f32[1,2,8,1024]{3,2,1,0:T(8,128)S(1)}, f32[1,2,8,1024]{3,2,1,0:T(8,128)S(1)}, u32[]{:S(2)}, u32[]{:S(2)}) collective-permute-start(f32[1,2,8,1024]{3,2,1,0:T(8,128)S(1)} %get-tuple-element.82), channel_id=1, source_target_pairs={{0,4},{4,8},{8,12},{1,5},{5,9},{9,13},{2,6},{6,10},{10,14},{3,7},{... | collective-permute-start | bytes 196616 | tf_op jit(solution)/shard_map/ppermute | solution.py:29
  96.1 6.2 %collective-permute-start.26 = (f32[1,2,8,1024]{3,2,1,0:T(8,128)S(1)}, f32[1,2,8,1024]{3,2,1,0:T(8,128)S(1)}, u32[]{:S(2)}, u32[]{:S(2)}) collective-permute-start(f32[1,2,8,1024]{3,2,1,0:T(8,128)S(1)} %get-tuple-element.83), channel_id=1, source_target_pairs={{4,0},{8,4},{12,8},{5,1},{9,5},{13,9},{6,2},{10,6},{14,10},{7,3},{... | collective-permute-start | bytes 196616 | tf_op jit(solution)/shard_map/ppermute | solution.py:29
  102.3 6.1 %collective-permute-start.9 = (f32[1,4,2,1024]{3,2,1,0:T(2,128)S(1)}, f32[1,4,2,1024]{3,2,1,0:T(2,128)S(1)}, u32[]{:S(2)}, u32[]{:S(2)}) collective-permute-start(f32[1,4,2,1024]{3,2,1,0:T(2,128)S(1)} %get-tuple-element.90), channel_id=1, source_target_pairs={{0,1},{1,2},{2,3},{4,5},{5,6},{6,7},{8,9},{9,10},{10,11},{12,13},{... | collective-permute-start | bytes 98312 | tf_op jit(solution)/shard_map/ppermute | solution.py:20
  112.7 6.2 %collective-permute-start.12 = (f32[1,2,8,1024]{3,2,1,0:T(8,128)S(1)}, f32[1,2,8,1024]{3,2,1,0:T(8,128)S(1)}, u32[]{:S(2)}, u32[]{:S(2)}) collective-permute-start(f32[1,2,8,1024]{3,2,1,0:T(8,128)S(1)} %get-tuple-element.87), channel_id=1, source_target_pairs={{4,0},{8,4},{12,8},{5,1},{9,5},{13,9},{6,2},{10,6},{14,10},{7,3},{... | collective-permute-start | bytes 196616 | tf_op jit(solution)/shard_map/ppermute | solution.py:29
  114.2 6.4 %collective-permute-start.11 = (f32[1,2,8,1024]{3,2,1,0:T(8,128)S(1)}, f32[1,2,8,1024]{3,2,1,0:T(8,128)S(1)}, u32[]{:S(2)}, u32[]{:S(2)}) collective-permute-start(f32[1,2,8,1024]{3,2,1,0:T(8,128)S(1)} %get-tuple-element.86), channel_id=1, source_target_pairs={{0,4},{4,8},{8,12},{1,5},{5,9},{9,13},{2,6},{6,10},{10,14},{3,7},{... | collective-permute-start | bytes 196616 | tf_op jit(solution)/shard_map/ppermute | solution.py:29
  (4 other events, 27.3 us)
where the time goes:
time: 134 us; the launch traced here: 132 us
  starting transfers between devices  75.4 us (56%)
  waiting for transfers between devices  21.3 us (16%)
  other arithmetic  16.3 us (12%)
  between operations  15.9 us (12%)
  local copies, waits for them, and re-layouts  2.77 us (2%)
    ppermute x15, starting transfers between devices, shifted_2(): lax.ppermute(value, axis, [(source, source + steps) for source in range(i...  39.4 us
    ppermute x6, starting transfers between devices, extended(): before = lax.ppermute(last, axis, up)  28.2 us
    ppermute x15, waiting for transfers between devices, shifted_2(): lax.ppermute(value, axis, [(source, source + steps) for source in range(i...  11.2 us
    ppermute x6, waiting for transfers between devices, extended(): after = lax.ppermute(initial, axis, down)  9.41 us
    ppermute x6, starting transfers between devices, extended(): after = lax.ppermute(initial, axis, down)  7.75 us
    mul x4, other arithmetic, attributes(): 0.25 * (neighbor(tensor, which_axis + 1, 1, up_open) + 2.0 * tensor + nei...  4.43 us
  transfers between devices with their start and end apart: 27, of which 10 were waited for; matrix products, arithmetic and copies ran while one was open for 6% of the time, Pallas kernels for 0%

commit v1 on v0

v1 whole, which is shorter than its diff:
```python
import jax
import jax.numpy as jnp
from jax import lax
from jax.experimental import pallas as pl
from jax.experimental.pallas import tpu as pltpu
from jax.sharding import PartitionSpec as P

MESH = pl.DeviceIdType.MESH
step_size = 0.15
epsilon = 1e-06
half_step = 0.5 * step_size
SUB, LANE = 8, 128

LEFT, RIGHT, ABOVE, BELOW = (0, -1), (0, 1), (-1, 0), (1, 0)
DIRS = [LEFT, RIGHT, ABOVE, BELOW, (-1, -1), (-1, 1), (1, -1), (1, 1)]


def slots(side, corner):
    table, at = {}, 0
    for d in DIRS:
        n = corner if d[0] and d[1] else side
        table[d] = (at, n)
        at += n
    return table, at


FIRST, FIRST_LEN = slots(14, 3)
SECOND, SECOND_LEN = slots(8, 3)


def positions():
    lane = lax.broadcasted_iota(jnp.int32, (SUB, LANE), 1)
    sub = lax.broadcasted_iota(jnp.int32, (SUB, LANE), 0)
    return lane == 0, lane == LANE - 1, (lane == 0) & (sub == 0), (lane == LANE - 1) & (sub == SUB - 1)


def later(v, pos):
    n = v.ndim
    rolled = pltpu.roll(v, LANE - 1, n - 1)
    v_next = jnp.where(pos[1], pltpu.roll(rolled, SUB - 1, n - 2), rolled)
    return jnp.where(pos[3], v, v_next)


def around(v, pos):
    n = v.ndim
    rolled = pltpu.roll(v, 1, n - 1)
    return jnp.where(pos[0], pltpu.roll(rolled, 1, n - 2), rolled)


def earlier(v, pos):
    return jnp.where(pos[2], v, around(v, pos))


def pad_rows(value, before, after):
    zero = jnp.zeros((1,) + value.shape[1:], value.dtype)
    return jnp.concatenate([zero] * before + [value] + [zero] * after, 0)


def pad_cols(value, before, after):
    zero = jnp.zeros((value.shape[0], 1) + value.shape[2:], value.dtype)
    return jnp.concatenate([zero] * before + [value] + [zero] * after, 1)


def kernel(widths_ref, survey_ref, conduct_ref, coh_ref, curv_ref, raw_u, raw_k, send1, recv1, send2, recv2, load_sem, out1, in1, out2, in2):
    batch = lax.axis_index("segment")
    i, n_i = lax.axis_index("inline"), lax.axis_size("inline")
    x, n_x = lax.axis_index("xline"), lax.axis_size("xline")
    has = {LEFT: x > 0, RIGHT: x < n_x - 1, ABOVE: i > 0, BELOW: i < n_i - 1}

    def exists(d):
        parts = [has[part] for part in ((d[0], 0), (0, d[1])) if part != (0, 0)]
        return parts[0] if len(parts) == 1 else parts[0] & parts[1]

    def device(d):
        return {"inline": i + d[0], "xline": x + d[1]}

    load_u = pltpu.make_async_copy(survey_ref.at[batch], raw_u, load_sem.at[0])
    load_k = pltpu.make_async_copy(conduct_ref.at[:, batch], raw_k, load_sem.at[1])
    load_u.start()
    load_k.start()

    barrier = pltpu.get_barrier_semaphore()
    for d in DIRS:

        @pl.when(exists(d))
        def _():
            pl.semaphore_signal(barrier, inc=1, device_id=device(d), device_id_type=MESH)

    def copy(d, table, src, dst, out_sems, in_sems):
        back = (-d[0], -d[1])
        at, n = table[d]
        to, _ = table[back]
        return pltpu.make_async_remote_copy(
            src_ref=src.at[pl.ds(at, n)],
            dst_ref=dst.at[pl.ds(to, n)],
            send_sem=out_sems.at[DIRS.index(d)],
            recv_sem=in_sems.at[DIRS.index(back)],
            device_id=device(d),
            device_id_type=MESH,
        )

    def arrival(d, table, src, dst, out_sems, in_sems):
        at, n = table[d]
        return pltpu.make_async_remote_copy(
            src_ref=src.at[pl.ds(at, n)],
            dst_ref=dst.at[pl.ds(at, n)],
            send_sem=out_sems.at[DIRS.index(d)],
            recv_sem=in_sems.at[DIRS.index(d)],
            device_id=device(d),
            device_id_type=MESH,
        )

    pos = positions()
    width = widths_ref[batch, 0]
    is2, is3, is4 = width == 2, width == 3, width == 4

    def last(v):
        return jnp.where(is2, v[1:2], jnp.where(is3, v[2:3], v[3:4]))

    def at_last(v):
        zero = jnp.zeros_like(v)
        return jnp.concatenate([zero, jnp.where(is2, v, zero), jnp.where(is3, v, zero), jnp.where(is4, v, zero)], 0)

    load_u.wait()
    load_k.wait()
    rows, cols = raw_u.shape[0], raw_u.shape[1]
    shape = (rows, cols, SUB, LANE)
    u = raw_u[...].reshape(shape)
    ki, kx, kt = (raw_k[a].astype(jnp.float32).reshape(shape) for a in range(3))

    ct = kt + later(kt, pos)
    cx = kx[:, 1:] + kx[:, :-1]
    ci = ki[1:] + ki[:-1]
    ci = jnp.concatenate([ci[0:1], jnp.where(width > 2, ci[1:2], 0.0), jnp.where(width > 3, ci[2:3], 0.0)], 0)

    def inner(v):
        ft = ct * (later(v, pos) - v)
        fx = cx * (v[:, 1:] - v[:, :-1])
        fi = ci * (v[1:] - v[:-1])
        total = ft - around(ft, pos)
        total = total + pad_cols(fx, 0, 1) - pad_cols(fx, 1, 0)
        return total + pad_rows(fi, 0, 1) - pad_rows(fi, 1, 0)

    p = u + half_step * inner(u)

    def put(ref, at, value):
        ref[pl.ds(at, value.shape[0])] = value

    ki_last, u_last, kx_last, p_last = last(ki)[0], last(u)[0], last(kx)[0], last(p)[0]
    for d, c in ((LEFT, 0), (RIGHT, cols - 1)):
        at = FIRST[d][0]
        put(send1, at, p[:, c])
        put(send1, at + 4, u[:, c])
        put(send1, at + 8, kx[:, c])
        put(send1, at + 12, ki[0, c : c + 1])
        put(send1, at + 13, ki_last[c : c + 1])
    for d, (pr, ur, kir, kxr) in ((ABOVE, (p[0], u[0], ki[0], kx[0])), (BELOW, (p_last, u_last, ki_last, kx_last))):
        at = FIRST[d][0]
        put(send1, at, pr)
        put(send1, at + 4, ur)
        put(send1, at + 8, kir)
        put(send1, at + 12, kxr[0:1])
        put(send1, at + 13, kxr[cols - 1 :])
        for dx, c in ((-1, 0), (1, cols - 1)):
            at = FIRST[(d[0], dx)][0]
            put(send1, at, ur[c : c + 1])
            put(send1, at + 1, kir[c : c + 1])
            put(send1, at + 2, kxr[c : c + 1])

    expected = (1 + has[LEFT].astype(jnp.int32) + has[RIGHT].astype(jnp.int32)) * (
        1 + has[ABOVE].astype(jnp.int32) + has[BELOW].astype(jnp.int32)
    ) - 1
    pl.semaphore_wait(barrier, expected)

    def send_all(*what):
        for d in DIRS:

            @pl.when(exists(d))
            def _():
                copy(d, *what).start()

    def receive_all(*what):
        for d in DIRS:

            @pl.when(exists(d))
            def _():
                arrival(d, *what).wait_recv()

    def drain(*what):
        for d in DIRS:

            @pl.when(exists(d))
            def _():
                copy(d, *what).wait_send()

    one = (FIRST, send1, recv1, out1, in1)
    two = (SECOND, send2, recv2, out2, in2)
    send_all(*one)
    receive_all(*one)

    def got(d, at, n):
        return recv1[pl.ds(FIRST[d][0] + at, n)]

    def open_to(d, flux):
        return jnp.where(has[d], flux, 0.0)

    side_c, side_u1, side_flux = {}, {}, {}
    for d, c in ((LEFT, 0), (RIGHT, cols - 1)):
        p_d, u_d, kx_d = (got(d, at, rows)[:, None] for at in (0, 4, 8))
        side_c[d] = kx_d + kx[:, c : c + 1]
        flux = open_to(d, side_c[d] * (u_d - u[:, c : c + 1]))
        side_flux[d] = flux
        change = -flux
        corner = (-1, d[1])
        end = open_to(ABOVE, (got(corner, 1, 1) + got(d, 12, 1)) * (got(corner, 0, 1) - u_d[0]))
        change = change + pad_rows(end[None], 0, rows - 1)
        corner = (1, d[1])
        end = open_to(BELOW, (got(corner, 1, 1) + got(d, 13, 1)) * (got(corner, 0, 1) - last(u_d)[0]))
        change = change + at_last(end[None])
        side_u1[d] = p_d + half_step * change
    for d, (ki_r, u_r) in ((ABOVE, (ki[0:1], u[0:1])), (BELOW, (ki_last[None], u_last[None]))):
        p_d, u_d, ki_d = (got(d, at, cols)[None] for at in (0, 4, 8))
        side_c[d] = ki_d + ki_r
        flux = open_to(d, side_c[d] * (u_d - u_r))
        side_flux[d] = flux
        change = -flux
        corner = (d[0], -1)
        end = open_to(LEFT, (got(corner, 2, 1) + got(d, 12, 1)) * (got(corner, 0, 1) - u_d[0, 0:1]))
        change = change + pad_cols(end[None], 0, cols - 1)
        corner = (d[0], 1)
        end = open_to(RIGHT, (got(corner, 2, 1) + got(d, 13, 1)) * (got(corner, 0, 1) - u_d[0, cols - 1 :]))
        change = change + pad_cols(end[None], cols - 1, 0)
        side_u1[d] = p_d + half_step * change

    def outer(flux):
        return (
            pad_cols(flux[LEFT], 0, cols - 1)
            + pad_cols(flux[RIGHT], cols - 1, 0)
            + pad_rows(flux[ABOVE], 0, rows - 1)
            + at_last(flux[BELOW])
        )

    u1 = p + half_step * outer(side_flux)
    u1_edge = {LEFT: u1[:, 0:1], RIGHT: u1[:, cols - 1 :], ABOVE: u1[0:1], BELOW: last(u1)}
    flux2 = {d: open_to(d, side_c[d] * (side_u1[d] - u1_edge[d])) for d in u1_edge}
    u2 = u1 + half_step * (inner(u1) + outer(flux2))

    top = u2[0:2]
    bottom = jnp.where(is2, u2[0:2], jnp.where(is3, u2[1:3], u2[2:4]))

    def flat(v):
        return v.reshape((v.shape[0] * v.shape[1], SUB, LANE))

    put(send2, SECOND[LEFT][0], flat(u2[:, 0:2]))
    put(send2, SECOND[RIGHT][0], flat(u2[:, cols - 2 :]))
    put(send2, SECOND[ABOVE][0], flat(top))
    put(send2, SECOND[BELOW][0], flat(bottom))
    for dx, near, far in ((-1, 0, 1), (1, cols - 1, cols - 2)):
        for di, block, r_near, r_far in ((-1, top, 0, 1), (1, bottom, 1, 0)):
            at = SECOND[(di, dx)][0]
            put(send2, at, block[r_near, near : near + 1])
            put(send2, at + 1, block[r_near, far : far + 1])
            put(send2, at + 2, block[r_far, near : near + 1])
    send_all(*two)
    receive_all(*two)

    def block2(d, r, c):
        return recv2[pl.ds(SECOND[d][0], r * c)].reshape((r, c, SUB, LANE))

    def corner2(d):
        at = SECOND[d][0]
        near, side, row = (recv2[pl.ds(at + j, 1)][None] for j in range(3))
        near_row = [side, near] if d[1] < 0 else [near, side]
        far_row = [row, row]
        near_row, far_row = jnp.concatenate(near_row, 1), jnp.concatenate(far_row, 1)
        return jnp.concatenate([far_row, near_row] if d[0] < 0 else [near_row, far_row], 0)

    own = jnp.concatenate([block2(LEFT, rows, 2), u2, block2(RIGHT, rows, 2)], 1)
    above = jnp.concatenate([corner2((-1, -1)), block2(ABOVE, 2, cols), corner2((-1, 1))], 1)
    below = jnp.concatenate([corner2((1, -1)), block2(BELOW, 2, cols), corner2((1, 1))], 1)
    b0, b1 = below[0:1], below[1:2]
    e = [
        above[0:1],
        jnp.where(has[ABOVE], above[1:2], own[0:1]),
        own[0:1],
        own[1:2],
        jnp.where(is2, b0, own[2:3]),
        jnp.where(is2, b1, jnp.where(is3, b0, own[3:4])),
        jnp.where(is3, b1, b0),
        b1,
    ]
    no_next = jnp.logical_not(has[BELOW])
    closes = {4: no_next & is2, 5: no_next & is3, 6: no_next & is4}

    def close_rows(r):
        return [jnp.where(closes[j], r[j - 1], r[j]) if j in closes else r[j] for j in range(len(r))]

    e = jnp.concatenate(close_rows(e), 0)
    e = jnp.concatenate(
        [
            e[:, 0:1],
            jnp.where(has[LEFT], e[:, 1:2], e[:, 2:3]),
            e[:, 2:6],
            jnp.where(has[RIGHT], e[:, 6:7], e[:, 5:6]),
            e[:, 7:8],
        ],
        1,
    )
    mid = e[1:7, 1:7]
    gi = e[2:8, 1:7] - e[0:6, 1:7]
    gx = e[1:7, 2:8] - e[1:7, 0:6]
    gt = later(mid, pos) - earlier(mid, pos)

    def close(g):
        r = [None] + [g[j : j + 1] for j in range(6)]
        r[1] = jnp.where(has[ABOVE], r[1], r[2])
        g = jnp.concatenate(close_rows(r)[1:], 0)
        return jnp.concatenate(
            [jnp.where(has[LEFT], g[:, 0:1], g[:, 1:2]), g[:, 1:5], jnp.where(has[RIGHT], g[:, 5:6], g[:, 4:5])], 1
        )

    gi, gx, gt = close(gi), close(gx), close(gt)

    def smoothed(v):
        v = v[0:5] + v[1:6]
        v = v[0:4] + v[1:5]
        v = v[:, 0:5] + v[:, 1:6]
        v = v[:, 0:4] + v[:, 1:5]
        return (1.0 / 256.0) * (later(v, pos) + 2.0 * v + earlier(v, pos))

    j11, j22, j33 = smoothed(gi * gi), smoothed(gx * gx), smoothed(gt * gt)
    j12, j13, j23 = smoothed(gi * gx), smoothed(gi * gt), smoothed(gx * gt)
    trace = j11 + j22 + j33
    minors = j11 * j22 - j12 * j12 + j11 * j33 - j13 * j13 + j22 * j33 - j23 * j23
    coherence = 1.0 - 3.0 * minors / (trace * trace + epsilon)
    gi, gx = gi[1:5, 1:5], gx[1:5, 1:5]
    inside = e[2:6, 2:6]
    second = e[3:7, 2:6] + e[1:5, 2:6] + e[2:6, 3:7] + e[2:6, 1:5] - 4.0 * inside
    root = lax.rsqrt(1.0 + 0.25 * (gi * gi + gx * gx))
    curvature = second * (root * root * root)
    for r in range(rows):
        coh_ref[r] = jnp.where(r < width, coherence[r], 0.0)
        curv_ref[r] = jnp.where(r < width, curvature[r], 0.0)
    drain(*one)
    drain(*two)


def on_device(survey, conduct, widths):
    _, rows, cols, samples = survey.shape
    traces = jax.ShapeDtypeStruct((rows, cols, SUB, LANE), jnp.float32)
    vmem = pl.BlockSpec(memory_space=pltpu.VMEM)
    hbm = pl.BlockSpec(memory_space=pl.ANY)
    buffer = lambda n: pltpu.VMEM((n, SUB, LANE), jnp.float32)
    coherence, curvature = pl.pallas_call(
        kernel,
        out_shape=(traces, traces),
        in_specs=[pl.BlockSpec(memory_space=pltpu.SMEM), hbm, hbm],
        out_specs=(vmem, vmem),
        scratch_shapes=[
            pltpu.VMEM((rows, cols, samples), jnp.float32),
            pltpu.VMEM((3, rows, cols, samples), jnp.bfloat16),
            buffer(FIRST_LEN),
            buffer(FIRST_LEN),
            buffer(SECOND_LEN),
            buffer(SECOND_LEN),
            pltpu.SemaphoreType.DMA((2,)),
            pltpu.SemaphoreType.DMA((8,)),
            pltpu.SemaphoreType.DMA((8,)),
            pltpu.SemaphoreType.DMA((8,)),
            pltpu.SemaphoreType.DMA((8,)),
        ],
        compiler_params=pltpu.CompilerParams(
            collective_id=0, has_side_effects=True, vmem_limit_bytes=32 * 1024 * 1024
        ),
    )(widths, survey, conduct)
    shape = (1, rows, cols, samples)
    return coherence.reshape(shape), curvature.reshape(shape)


def solution(mesh):
    placed = (
        P(None, "inline", "xline", None),
        P(None, None, "inline", "xline", None),
        P(None, "inline"),
    )
    return jax.shard_map(
        on_device,
        mesh=mesh,
        in_specs=placed,
        out_specs=(P("segment", "inline", "xline", None), P("segment", "inline", "xline", None)),
        check_vma=False,
    )
```

time: 134 us -> 19.7 us (0.15); the launches traced: 132 us -> 19.6 us
  starting transfers between devices: 75.4 us -> 0 us
  waiting for transfers between devices: 21.3 us -> 0 us
  other arithmetic: 16.3 us -> 0 us
  between operations: 15.9 us -> 0.64 us
  Pallas kernels: 0 us -> 15 us
    ppermute x27 -> x0, starting transfers between devices: 75.4 us -> none  [the longest x15 39.4 us: shifted_2(): lax.ppermute(value, axis, [(source, source + steps) for source in range(i...]
    ppermute x27 -> x0, waiting for transfers between devices: 21.3 us -> none  [the longest x15 11.2 us: shifted_2(): lax.ppermute(value, axis, [(source, source + steps) for source in range(i...]
    pallas_call x0 -> x1, Pallas kernels: none -> 15 us  [on_device(): pl.pallas_call(kernel, out_shape=(traces, traces), in_specs=[pl.BlockSpec...]
    mul x4 -> x0, other arithmetic: 4.43 us -> none  [attributes(): 0.25 * (neighbor(tensor, which_axis + 1, 1, up_open) + 2.0 * tensor + nei...]
    not x7 -> x0, other arithmetic: 2.67 us -> none  [the longest x4 2.63 us: face_masks(): jnp.logical_not(last_row & (own_row == width) | first_row & (own_row == 0))]
    unnamed x2 -> x5, local copies, waits for them, and re-layouts: 0.01 us -> 2.57 us
    add x9 -> x0, other arithmetic: 2.14 us -> none  [the longest x4 1.2 us: relax_step(): change + 0.5 * (kk + neighbor(kk, which_axis, offset, opened)) * (neighbo...]
    slice x4 -> x0, local copies, waits for them, and re-layouts: 1.38 us -> none  [the longest x1 0.66 us: on_device(): results.append(attributes(arrived, widths[batch, 0]))]
  transfers between devices with their start and end apart: 27 -> 0, of which waited for: 10 -> 0; matrix products, arithmetic and copies ran while one was open for 6% -> 0% of each run, Pallas kernels for 0% -> 0%
where the time goes in v1:
time: 19.7 us; the launch traced here: 19.6 us
  Pallas kernels  15 us (76%)
  local copies, waits for them, and re-layouts  3.88 us (20%)
  between operations  0.64 us (3%)
    pallas_call x1, Pallas kernels, on_device(): pl.pallas_call(kernel, out_shape=(traces, traces), in_specs=[pl.BlockSpec...  15 us
    unnamed x5, local copies, waits for them, and re-layouts  2.57 us
    reshape x2, local copies, waits for them, and re-layouts, on_device(): return (coherence.reshape(shape), curvature.reshape(shape))  1.3 us

profile of v1, /device:TPU:0, one launch (start us, length us, event | category | flops | bytes accessed | tf_op | source)
XLA Modules:
  0.0 19.6 jit_solution(11568785849433522350)
XLA Ops:
  0.6 0.7 %copy.5.widths_ref = s32[2,1]{1,0:T(2,128)S(1)} copy(s32[2,1]{0,1:T(1,128)} %param.5) | data formatting | bytes 16 | tf_op args[2]
  1.4 0.0 copy-start
  1.4 0.9 %copy-done = bf16[3,2,4,4,1024]{4,3,2,1,0:T(4,128)(2,1)S(1)} copy-done((bf16[3,2,4,4,1024]{4,3,2,1,0:T(4,128)(2,1)S(1)}, bf16[3,2,4,4,1024]{4,3,2,1,0:T(4,128)(2,1)}, u32[]{:S(2)}) %copy-start) | copy-done | bytes 196632
  2.3 0.0 copy-start.1
  2.3 0.9 %copy-done.1 = f32[2,4,4,1024]{3,2,1,0:T(4,128)S(1)} copy-done((f32[2,4,4,1024]{3,2,1,0:T(4,128)S(1)}, f32[2,4,4,1024]{3,2,1,0:T(4,128)}, u32[]{:S(2)}) %copy-start.1) | copy-done | bytes 131096
  3.2 15.0 %shard_map.50 = (f32[4,4,8,128]{3,2,1,0:T(8,128)S(1)}, f32[4,4,8,128]{3,2,1,0:T(8,128)S(1)}) custom-call(s32[2,1]{1,0:T(2,128)S(1)} %copy.5.widths_ref, f32[2,4,4,1024]{3,2,1,0:T(4,128)S(1)} %copy-done.1, bf16[3,2,4,4,1024]{4,3,2,1,0:T(4,128)(2,1)S(1)} %copy-done), custom_call_target="tpu_custom_call" | custom-call | tf_op jit(solution)/shard_map/pallas_call | solution.py:354
  18.3 0.7 %reshape.10 = f32[1,4,4,1024]{3,2,1,0:T(4,128)} reshape(f32[4,4,8,128]{3,2,1,0:T(8,128)S(1)} %get-tuple-element.4) | data formatting | bytes 131072 | tf_op jit(solution)/shard_map/reshape | solution.py:377
  18.9 0.7 %reshape.11 = f32[1,4,4,1024]{3,2,1,0:T(4,128)} reshape(f32[4,4,8,128]{3,2,1,0:T(8,128)S(1)} %get-tuple-element.5) | data formatting | bytes 131072 | tf_op jit(solution)/shard_map/reshape | solution.py:377
Async XLA Ops:
  1.4 0.9 %copy-start = (bf16[3,2,4,4,1024]{4,3,2,1,0:T(4,128)(2,1)S(1)}, bf16[3,2,4,4,1024]{4,3,2,1,0:T(4,128)(2,1)}, u32[]{:S(2)}) copy-start(bf16[3,2,4,4,1024]{4,3,2,1,0:T(4,128)(2,1)} %conduct_ref.1) | copy-start | bytes 589828
  2.3 0.9 %copy-start.1 = (f32[2,4,4,1024]{3,2,1,0:T(4,128)S(1)}, f32[2,4,4,1024]{3,2,1,0:T(4,128)}, u32[]{:S(2)}) copy-start(f32[2,4,4,1024]{3,2,1,0:T(4,128)} %survey_ref.1) | copy-start | bytes 393220

commit v2 on v1

--- a/solution.py
+++ b/solution.py
@@ -12,7 +12,7 @@
 SUB, LANE = 8, 128
 
 LEFT, RIGHT, ABOVE, BELOW = (0, -1), (0, 1), (-1, 0), (1, 0)
-DIRS = [LEFT, RIGHT, ABOVE, BELOW, (-1, -1), (-1, 1), (1, -1), (1, 1)]
+DIRS = [(-1, -1), (-1, 1), (1, -1), (1, 1), LEFT, RIGHT, ABOVE, BELOW]
 
 
 def slots(side, corner):
@@ -111,7 +111,7 @@
         )
 
     pos = positions()
-    width = widths_ref[batch, 0]
+    width = widths_ref[0, batch]
     is2, is3, is4 = width == 2, width == 3, width == 4
 
     def last(v):
@@ -370,9 +370,9 @@
             pltpu.SemaphoreType.DMA((8,)),
         ],
         compiler_params=pltpu.CompilerParams(
-            collective_id=0, has_side_effects=True, vmem_limit_bytes=32 * 1024 * 1024
+            collective_id=0, has_side_effects=True, vmem_limit_bytes=55000 * 1024
         ),
-    )(widths, survey, conduct)
+    )(widths.T, survey, conduct)
     shape = (1, rows, cols, samples)
     return coherence.reshape(shape), curvature.reshape(shape)
 

time: 19.7 us -> 17.1 us (0.87)
  local copies, waits for them, and re-layouts: 3.88 us -> 1.95 us
  Pallas kernels: 15 us -> 14.3 us
    unnamed x5 -> x2, local copies, waits for them, and re-layouts: 2.57 us -> 0.65 us
    pallas_call x1, Pallas kernels: 15 us -> 14.3 us  [on_device(): pl.pallas_call(kernel, out_shape=(traces, traces), in_specs=[pl.BlockSpec...]
where the time goes in v2:
time: 17.1 us; the launch traced here: 16.9 us
  Pallas kernels  14.3 us (84%)
  local copies, waits for them, and re-layouts  1.95 us (11%)
  between operations  0.65 us (4%)
    pallas_call x1, Pallas kernels, on_device(): pl.pallas_call(kernel, out_shape=(traces, traces), in_specs=[pl.BlockSpec...  14.3 us
    reshape x2, local copies, waits for them, and re-layouts, on_device(): return (coherence.reshape(shape), curvature.reshape(shape))  1.3 us
    unnamed x2, local copies, waits for them, and re-layouts  0.65 us

profile of v2, /device:TPU:0, one launch (start us, length us, event | category | flops | bytes accessed | tf_op | source)
XLA Modules:
  0.0 16.9 jit_solution(2233579809767339128)
XLA Ops:
  0.6 0.0 copy-start
  0.6 0.6 %copy-done = s32[2,1]{0,1:T(1,128)S(1)} copy-done((s32[2,1]{0,1:T(1,128)S(1)}, s32[2,1]{0,1:T(1,128)}, u32[]{:S(2)}) %copy-start) | copy-done | bytes 32
  1.3 14.3 %shard_map.50 = (f32[4,4,8,128]{3,2,1,0:T(8,128)S(1)}, f32[4,4,8,128]{3,2,1,0:T(8,128)S(1)}) custom-call(s32[1,2]{1,0:T(1,128)S(1)} %bitcast.5, f32[2,4,4,1024]{3,2,1,0:T(4,128)} %survey_ref.1, bf16[3,2,4,4,1024]{4,3,2,1,0:T(4,128)(2,1)} %conduct_ref.1), custom_call_target="tpu_custom_call" | custom-call | tf_op jit(solution)/shard_map/pallas_call | solution.py:354
  15.6 0.7 %reshape.10 = f32[1,4,4,1024]{3,2,1,0:T(4,128)} reshape(f32[4,4,8,128]{3,2,1,0:T(8,128)S(1)} %get-tuple-element.4) | data formatting | bytes 131072 | tf_op jit(solution)/shard_map/reshape | solution.py:377
  16.3 0.7 %reshape.11 = f32[1,4,4,1024]{3,2,1,0:T(4,128)} reshape(f32[4,4,8,128]{3,2,1,0:T(8,128)S(1)} %get-tuple-element.5) | data formatting | bytes 131072 | tf_op jit(solution)/shard_map/reshape | solution.py:377
Async XLA Ops:
  0.6 0.7 %copy-start = (s32[2,1]{0,1:T(1,128)S(1)}, s32[2,1]{0,1:T(1,128)}, u32[]{:S(2)}) copy-start(s32[2,1]{0,1:T(1,128)} %param.5) | copy-start | bytes 28

commit v3 on v2

--- a/solution.py
+++ b/solution.py
@@ -61,7 +61,7 @@
     return jnp.concatenate([zero] * before + [value] + [zero] * after, 1)
 
 
-def kernel(widths_ref, survey_ref, conduct_ref, coh_ref, curv_ref, raw_u, raw_k, send1, recv1, send2, recv2, load_sem, out1, in1, out2, in2):
+def kernel(widths_ref, survey_ref, conduct_ref, coh_ref, raw_u, raw_k, send1, recv1, send2, recv2, load_sem, out1, in1, out2, in2):
     batch = lax.axis_index("segment")
     i, n_i = lax.axis_index("inline"), lax.axis_size("inline")
     x, n_x = lax.axis_index("xline"), lax.axis_size("xline")
@@ -339,23 +339,23 @@
     root = lax.rsqrt(1.0 + 0.25 * (gi * gi + gx * gx))
     curvature = second * (root * root * root)
     for r in range(rows):
-        coh_ref[r] = jnp.where(r < width, coherence[r], 0.0)
-        curv_ref[r] = jnp.where(r < width, curvature[r], 0.0)
+        coh_ref[0, r] = jnp.where(r < width, coherence[r], 0.0).reshape((cols, SUB * LANE))
+        coh_ref[1, r] = jnp.where(r < width, curvature[r], 0.0).reshape((cols, SUB * LANE))
     drain(*one)
     drain(*two)
 
 
 def on_device(survey, conduct, widths):
     _, rows, cols, samples = survey.shape
-    traces = jax.ShapeDtypeStruct((rows, cols, SUB, LANE), jnp.float32)
+    traces = jax.ShapeDtypeStruct((2, rows, cols, samples), jnp.float32)
     vmem = pl.BlockSpec(memory_space=pltpu.VMEM)
     hbm = pl.BlockSpec(memory_space=pl.ANY)
     buffer = lambda n: pltpu.VMEM((n, SUB, LANE), jnp.float32)
-    coherence, curvature = pl.pallas_call(
+    both = pl.pallas_call(
         kernel,
-        out_shape=(traces, traces),
+        out_shape=traces,
         in_specs=[pl.BlockSpec(memory_space=pltpu.SMEM), hbm, hbm],
-        out_specs=(vmem, vmem),
+        out_specs=vmem,
         scratch_shapes=[
             pltpu.VMEM((rows, cols, samples), jnp.float32),
             pltpu.VMEM((3, rows, cols, samples), jnp.bfloat16),
@@ -373,8 +373,7 @@
             collective_id=0, has_side_effects=True, vmem_limit_bytes=55000 * 1024
         ),
     )(widths.T, survey, conduct)
-    shape = (1, rows, cols, samples)
-    return coherence.reshape(shape), curvature.reshape(shape)
+    return both[0:1], both[1:2]
 
 
 def solution(mesh):

time: 17.1 us -> 16.4 us (0.959)
  local copies, waits for them, and re-layouts: 1.95 us -> 1.31 us
    reshape x2 -> x0, local copies, waits for them, and re-layouts: 1.3 us -> none  [on_device(): return (coherence.reshape(shape), curvature.reshape(shape))]
    slice x0 -> x1, local copies, waits for them, and re-layouts: none -> 0.66 us  [on_device(): return (both[0:1], both[1:2])]
where the time goes in v3:
time: 16.4 us; the launch traced here: 16.3 us
  Pallas kernels  14.3 us (87%)
  local copies, waits for them, and re-layouts  1.31 us (8%)
  between operations  0.65 us (4%)
    pallas_call x1, Pallas kernels, on_device(): pl.pallas_call(kernel, out_shape=traces, in_specs=[pl.BlockSpec(memory_sp...  14.3 us
    slice x1, local copies, waits for them, and re-layouts, on_device(): return (both[0:1], both[1:2])  0.66 us
    unnamed x2, local copies, waits for them, and re-layouts  0.65 us

profile of v3, /device:TPU:0, one launch (start us, length us, event | category | flops | bytes accessed | tf_op | source)
XLA Modules:
  0.0 16.3 jit_solution(14667191662733325047)
XLA Ops:
  0.6 0.0 copy-start
  0.6 0.6 %copy-done = s32[2,1]{0,1:T(1,128)S(1)} copy-done((s32[2,1]{0,1:T(1,128)S(1)}, s32[2,1]{0,1:T(1,128)}, u32[]{:S(2)}) %copy-start) | copy-done | bytes 32
  1.3 14.3 %shard_map.50 = f32[2,4,4,1024]{3,2,1,0:T(4,128)S(1)} custom-call(s32[1,2]{1,0:T(1,128)S(1)} %bitcast.1, f32[2,4,4,1024]{3,2,1,0:T(4,128)} %survey_ref.1, bf16[3,2,4,4,1024]{4,3,2,1,0:T(4,128)(2,1)} %conduct_ref.1), custom_call_target="tpu_custom_call" | custom-call | tf_op jit(solution)/shard_map/pallas_call | solution.py:354
  15.6 0.7 %fusion = (f32[1,4,4,1024]{3,2,1,0:T(4,128)}, f32[1,4,4,1024]{3,2,1,0:T(4,128)}) fusion(f32[2,4,4,1024]{3,2,1,0:T(4,128)S(1)} %shard_map.50), kind=kLoop, calls=%fused_computation | loop fusion | bytes 262144 | tf_op jit(solution)/shard_map/slice | solution.py:376
Async XLA Ops:
  0.6 0.7 %copy-start = (s32[2,1]{0,1:T(1,128)S(1)}, s32[2,1]{0,1:T(1,128)}, u32[]{:S(2)}) copy-start(s32[2,1]{0,1:T(1,128)} %param.5) | copy-start | bytes 28

commit v4 on v3

--- a/solution.py
+++ b/solution.py
@@ -76,15 +76,15 @@
 
     load_u = pltpu.make_async_copy(survey_ref.at[batch], raw_u, load_sem.at[0])
     load_k = pltpu.make_async_copy(conduct_ref.at[:, batch], raw_k, load_sem.at[1])
-    load_u.start()
-    load_k.start()
-
     barrier = pltpu.get_barrier_semaphore()
     for d in DIRS:
 
         @pl.when(exists(d))
         def _():
             pl.semaphore_signal(barrier, inc=1, device_id=device(d), device_id_type=MESH)
+
+    load_u.start()
+    load_k.start()
 
     def copy(d, table, src, dst, out_sems, in_sems):
         back = (-d[0], -d[1])

time: 16.4 us -> 16.4 us (level)
  no operation moved by 1% of the time
where the time goes in v4:
time: 16.4 us; the launch traced here: 16.3 us
  Pallas kernels  14.3 us (87%)
  local copies, waits for them, and re-layouts  1.31 us (8%)
  between operations  0.65 us (4%)
    pallas_call x1, Pallas kernels, on_device(): pl.pallas_call(kernel, out_shape=traces, in_specs=[pl.BlockSpec(memory_sp...  14.3 us
    slice x1, local copies, waits for them, and re-layouts, on_device(): return (both[0:1], both[1:2])  0.66 us
    unnamed x2, local copies, waits for them, and re-layouts  0.65 us

profile of v4, /device:TPU:0, one launch (start us, length us, event | category | flops | bytes accessed | tf_op | source)
XLA Modules:
  0.0 16.3 jit_solution(4436434341627763182)
XLA Ops:
  0.6 0.0 copy-start
  0.6 0.6 %copy-done = s32[2,1]{0,1:T(1,128)S(1)} copy-done((s32[2,1]{0,1:T(1,128)S(1)}, s32[2,1]{0,1:T(1,128)}, u32[]{:S(2)}) %copy-start) | copy-done | bytes 32
  1.3 14.3 %shard_map.50 = f32[2,4,4,1024]{3,2,1,0:T(4,128)S(1)} custom-call(s32[1,2]{1,0:T(1,128)S(1)} %bitcast.1, f32[2,4,4,1024]{3,2,1,0:T(4,128)} %survey_ref.1, bf16[3,2,4,4,1024]{4,3,2,1,0:T(4,128)(2,1)} %conduct_ref.1), custom_call_target="tpu_custom_call" | custom-call | tf_op jit(solution)/shard_map/pallas_call | solution.py:354
  15.6 0.7 %fusion = (f32[1,4,4,1024]{3,2,1,0:T(4,128)}, f32[1,4,4,1024]{3,2,1,0:T(4,128)}) fusion(f32[2,4,4,1024]{3,2,1,0:T(4,128)S(1)} %shard_map.50), kind=kLoop, calls=%fused_computation | loop fusion | bytes 262144 | tf_op jit(solution)/shard_map/slice | solution.py:376
Async XLA Ops:
  0.6 0.7 %copy-start = (s32[2,1]{0,1:T(1,128)S(1)}, s32[2,1]{0,1:T(1,128)}, u32[]{:S(2)}) copy-start(s32[2,1]{0,1:T(1,128)} %param.5) | copy-start | bytes 28
